TPU v7x, 32 devices: a whole 2x2x4 slice. The times are simulated.
32 devices in a mesh: groups: 2 (over x), beam: 4 (over z), ctx: 4 (over y, core).
Axes of the slice: x: 2, y: 2, z: 4, core: 2. Of those that a mesh axis runs over, the one named last changes fastest.
Arguments:
- queries: bfloat16 [8, 16384], P(('groups', 'beam'), 'ctx'), parts along dimension 0
- new_keys: bfloat16 [8, 1024], P(('groups', 'beam')), parts along dimension 0, may hold values from -16 to 16
- new_values: bfloat16 [8, 1024], P(('groups', 'beam')), parts along dimension 0, may hold values from -9 to 9
- cache_keys: bfloat16 [8, 2048, 8, 128], P(('groups', 'beam'), 'ctx'), parts along dimension 0
- cache_values: bfloat16 [8, 2048, 8, 128], P(('groups', 'beam'), 'ctx'), parts along dimension 0, may hold values from -6 to 6
- parents: int32 [8], P('groups'), parts along dimension 0, may hold values from 0 to 3
- lengths: int32 [8], P('groups'), parts along dimension 0, may hold values from 8 to 16, as said below
- out_weight: bfloat16 [16384, 16384], P('ctx', 'beam'), may hold values from -0.046875 to 0.046875
Outputs:
- projected: bfloat16 [8, 16384], P('groups', ('beam', 'ctx')), parts along dimension 0
There are 2 independent parts, one for each index of `groups`. A program takes and returns all parts, laid end to end along the dimension named above; an argument that names none is the same for every part. Nothing has to cross between parts.
Inputs may be any that keep to these rules, and one draw needn't show every extreme that they name: `lengths`: each previous beam holds at least half of its 16 spans; in every draw some beam is full.
All inputs are finite; a program needn't handle non-finite values.
Results may differ from a plain program's by a relative error of at most 0.012.
Values may be sent and summed in bfloat16 or wider, within the bound.
A program may use at most 64 MiB of HBM per device.

v0:
```python
import math

import jax
import jax.numpy as jnp
from jax import lax
from jax.sharding import PartitionSpec as P

H = 128
KVH = 8
HD = 128
SPAN = 128


MASKED = -1e30


def shifted(array, axis, by):
    length = lax.axis_size(axis)
    return lax.ppermute(array, axis, [(i, (i + by) % length) for i in range(length)])


def local_partial(query_block, head_start, keys_here, values_here, usable):
    row_count = query_block.shape[0]
    head_count = query_block.shape[1]
    group_size = H // KVH
    kv_count = max(1, head_count // group_size)
    per_kv = min(head_count, group_size)
    kv_start = head_start // group_size
    key_heads = lax.dynamic_slice_in_dim(keys_here, kv_start, kv_count, 1)
    value_heads = lax.dynamic_slice_in_dim(values_here, kv_start, kv_count, 1)
    grouped = query_block.reshape(row_count, kv_count, per_kv, HD)
    scores = jnp.einsum("rkgd,tkd->rkgt", grouped, key_heads, preferred_element_type=jnp.float32)
    scores = scores * (1.0 / math.sqrt(HD))
    usable_mask = usable[:, None, None, :]
    scores = jnp.where(usable_mask, scores, MASKED)
    peak = jnp.max(scores, axis=-1)
    weights = jnp.where(usable_mask, jnp.exp(scores - peak[..., None]), 0.0)
    weight_sum = jnp.sum(weights, axis=-1)
    blended = jnp.einsum(
        "rkgt,tkd->rkgd",
        weights.astype(jnp.bfloat16),
        value_heads,
        preferred_element_type=jnp.float32,
    )
    return (
        peak.reshape(row_count, head_count),
        weight_sum.reshape(row_count, head_count),
        blended.reshape(row_count, head_count, HD),
    )


def own_token(query_block, head_start, key_rows, value_rows):
    row_count = query_block.shape[0]
    head_count = query_block.shape[1]
    group_size = H // KVH
    kv_count = max(1, head_count // group_size)
    per_kv = min(head_count, group_size)
    kv_start = head_start // group_size
    key_heads = lax.dynamic_slice_in_dim(
        key_rows.reshape(row_count, KVH, HD), kv_start, kv_count, 1
    )
    value_heads = lax.dynamic_slice_in_dim(
        value_rows.reshape(row_count, KVH, HD), kv_start, kv_count, 1
    )
    grouped = query_block.reshape(row_count, kv_count, per_kv, HD)
    own_score = jnp.einsum("rkgd,rkd->rkg", grouped, key_heads, preferred_element_type=jnp.float32)
    own_score = own_score * (1.0 / math.sqrt(HD))
    blended = jnp.broadcast_to(
        value_heads.astype(jnp.float32)[:, :, None, :], (row_count, kv_count, per_kv, HD)
    )
    return (
        own_score.reshape(row_count, head_count),
        jnp.ones((row_count, head_count), jnp.float32),
        blended.reshape(row_count, head_count, HD),
    )


def combine(earlier, later):
    peak = jnp.maximum(earlier[0], later[0])
    early_scale = jnp.exp(earlier[0] - peak)
    late_scale = jnp.exp(later[0] - peak)
    weight_sum = earlier[1] * early_scale + later[1] * late_scale
    blended = earlier[2] * early_scale[..., None] + later[2] * late_scale[..., None]
    return (peak, weight_sum, blended)


def per_device(
    queries, new_keys, new_values, cache_keys, cache_values, parents, lengths, out_weight
):
    ctx_count = lax.axis_size("ctx")
    ctx_index = lax.axis_index("ctx")
    beam_index = lax.axis_index("beam")
    local_tokens = cache_keys.shape[1]
    head_share = queries.shape[1] // HD
    row_query, row_key, row_value = (
        lax.all_gather(queries, "beam", axis=0, tiled=True),
        lax.all_gather(new_keys, "beam", axis=0, tiled=True),
        lax.all_gather(new_values, "beam", axis=0, tiled=True),
    )
    keys_here = cache_keys[0]
    values_here = cache_values[0]
    row_length = jnp.broadcast_to(lengths[beam_index], (row_query.shape[0],))
    row_keep = (parents == beam_index).astype(jnp.float32)
    row_count = row_query.shape[0]
    positions = ctx_index * local_tokens + jnp.arange(local_tokens, dtype=jnp.int32)
    usable = positions[None, :] < (row_length * SPAN)[:, None]
    home_start = ctx_index * head_share
    blocks = row_query.reshape(row_count, head_share, HD)
    home_state = own_token(blocks, home_start, row_key, row_value)

    def visit(visit_step, packet):
        anchor = (ctx_index - visit_step) % ctx_count
        partial_state = local_partial(
            packet[0], anchor * head_share, keys_here, values_here, usable
        )
        updated = combine((packet[1], packet[2], packet[3]), partial_state)
        moved_rows = shifted(packet[0], "ctx", 1)
        moved_state = shifted((updated[0], updated[1], updated[2]), "ctx", 1)
        return (moved_rows, moved_state[0], moved_state[1], moved_state[2])

    packet = lax.fori_loop(0, ctx_count, visit, (blocks,) + home_state)
    weight_sum = packet[2]
    blended = packet[3]
    result = (blended / weight_sum[..., None]).reshape(row_count, head_share * HD) * row_keep[
        :, None
    ]
    attended = lax.psum_scatter(result, "beam", scatter_dimension=0, tiled=True).astype(
        jnp.bfloat16
    )
    all_beams = lax.all_gather(attended, "beam", axis=0, tiled=True)
    partial_out = jnp.dot(all_beams, out_weight, preferred_element_type=jnp.float32)
    return lax.psum_scatter(partial_out, "ctx", scatter_dimension=1, tiled=True).astype(
        jnp.bfloat16
    )


def solution(mesh):
    placed = (
        P(("groups", "beam"), "ctx"),
        P(("groups", "beam"), None),
        P(("groups", "beam"), None),
        P(("groups", "beam"), "ctx", None, None),
        P(("groups", "beam"), "ctx", None, None),
        P("groups"),
        P("groups"),
        P("ctx", "beam"),
    )
    return jax.shard_map(
        per_device,
        mesh=mesh,
        in_specs=placed,
        out_specs=P("groups", ("beam", "ctx")),
        check_vma=False,
    )
```

profile of v0, /device:TPU:0, one launch (start us, length us, event | category | flops | bytes accessed | tf_op | source)
XLA Modules:
  0.0 166.2 jit_solution(13171231495237748360)
XLA Ops:
  7.2 14.9 %all-gather.1 = bf16[4,1,1024]{2,1,0:T(2,128)(2,1)S(1)} all-gather(bf16[1,1,1024]{2,1,0:T(2,128)(2,1)} %bitcast.86), channel_id=1, replica_groups=mesh['groups'=2,'beam'=4,'ctx'=4] {'beam'}, dimensions={0}, use_global_device_ids=true | all-gather | bytes 10240 | tf_op jit(solution)/shard_map/all_gather | solution.py:97
  22.2 13.3 %all-gather.2 = bf16[4,1,1024]{2,1,0:T(2,128)(2,1)S(1)} all-gather(bf16[1,1,1024]{2,1,0:T(2,128)(2,1)} %bitcast.87), channel_id=1, replica_groups=mesh['groups'=2,'beam'=4,'ctx'=4] {'beam'}, dimensions={0}, use_global_device_ids=true | all-gather | bytes 10240 | tf_op jit(solution)/shard_map/all_gather | solution.py:98
  35.6 13.4 %all-gather = bf16[4,1,4096]{2,1,0:T(2,128)(2,1)S(1)} all-gather(bf16[1,1,4096]{2,1,0:T(2,128)(2,1)} %bitcast.83), channel_id=1, replica_groups=mesh['groups'=2,'beam'=4,'ctx'=4] {'beam'}, dimensions={0}, use_global_device_ids=true | all-gather | bytes 40960 | tf_op jit(solution)/shard_map/all_gather | solution.py:96
  49.4 1.2 dynamic_slice.31
  51.2 1.9 %copy_bitcast_fusion = (bf16[512,8,128]{2,0,1:T(8,128)(2,1)S(1)}, bf16[512,8,128]{2,0,1:T(8,128)(2,1)S(1)}) fusion(bf16[1,512,8,128]{3,2,1,0:T(8,128)(2,1)} %param.14, bf16[1,512,8,128]{3,2,1,0:T(8,128)(2,1)} %param.13), kind=kLoop, calls=%fused_computation.25 | loop fusion | bytes 4194304 | tf_op jit(solution)/shard_map/squeeze | solution.py:101
  53.2 21.8 %while.22 = (s32[]{:T(128)}, bf16[4,32,128]{2,1,0:T(8,128)(2,1)S(1)}, f32[4,32]{1,0:T(4,128)S(1)}, f32[4,32]{1,0:T(4,128)S(1)}, f32[4,32,128]{2,1,0:T(8,128)S(1)...) while((s32[]{:T(128)}, ...), condition=%wide.region_3.4_spmd.clone, body=%wide.region_0.3_spmd.clone.sunk | while | flops 34193952 | bytes 2216578 | solution.py:121
  54.4 1.6 collective-permute-start
  56.6 2.4 %collective-permute-done.1 = f32[4,32]{1,0:T(4,128)S(1)} collective-permute-done((f32[4,32]{1,0:T(4,128)S(1)}, f32[4,32]{1,0:T(4,128)S(1)}, u32[]{:S(2)}, u32[]{:S(2)}) %collective-permute-start.1) | collective-permute-done | bytes 544 | tf_op jit(solution)/shard_map/while/body/eval_jaxpr/ppermute | solution.py:19
  60.2 1.0 collective-permute-start
  61.3 1.1 collective-permute-start.2
  62.4 1.8 %collective-permute-done.1 = f32[4,32]{1,0:T(4,128)S(1)} collective-permute-done((f32[4,32]{1,0:T(4,128)S(1)}, f32[4,32]{1,0:T(4,128)S(1)}, u32[]{:S(2)}, u32[]{:S(2)}) %collective-permute-start.1) | collective-permute-done | bytes 544 | tf_op jit(solution)/shard_map/while/body/eval_jaxpr/ppermute | solution.py:19
  65.4 1.2 collective-permute-start
  66.7 1.0 collective-permute-start.2
  67.7 2.0 %collective-permute-done.1 = f32[4,32]{1,0:T(4,128)S(1)} collective-permute-done((f32[4,32]{1,0:T(4,128)S(1)}, f32[4,32]{1,0:T(4,128)S(1)}, u32[]{:S(2)}, u32[]{:S(2)}) %collective-permute-start.1) | collective-permute-done | bytes 544 | tf_op jit(solution)/shard_map/while/body/eval_jaxpr/ppermute | solution.py:19
  70.9 1.0 collective-permute-start
  72.0 1.1 collective-permute-start.2
  73.1 1.8 %collective-permute-done.1 = f32[4,32]{1,0:T(4,128)S(1)} collective-permute-done((f32[4,32]{1,0:T(4,128)S(1)}, f32[4,32]{1,0:T(4,128)S(1)}, u32[]{:S(2)}, u32[]{:S(2)}) %collective-permute-start.1) | collective-permute-done | bytes 544 | tf_op jit(solution)/shard_map/while/body/eval_jaxpr/ppermute | solution.py:19
  75.2 19.6 %all-reduce = bf16[4,4096]{1,0:T(4,128)(2,1)S(1)} all-reduce(f32[4,4096]{1,0:T(4,128)S(1)} %bitcast_multiply_fusion.1), channel_id=2, replica_groups=mesh['groups'=2,'beam'=4,'ctx'=4] {'beam'}, use_global_device_ids=true, to_apply=%region_4.5.clone | all-reduce | flops 16384 | bytes 98304
  94.8 1.2 dynamic-slice
  96.0 0.7 fusion.21
  96.7 13.1 %all-gather.3 = bf16[4,1,4096]{2,1,0:T(2,128)(2,1)S(1)} all-gather(bf16[1,1,4096]{2,1,0:T(2,128)(2,1)S(1)} %fusion.21), channel_id=1, replica_groups=mesh['groups'=2,'beam'=4,'ctx'=4] {'beam'}, dimensions={0}, use_global_device_ids=true | all-gather | bytes 40960 | tf_op jit(solution)/shard_map/all_gather | solution.py:130
  109.8 18.2 %convolution_bitcast_fusion.1 = f32[4096,4]{1,0:T(8,128)} fusion(bf16[4096,4096]{1,0:T(8,128)(2,1)} %param.17, bf16[4,1,4096]{2,1,0:T(2,128)(2,1)S(1)} %all-gather.3), kind=kOutput, calls=%fused_computation.24 | convolution fusion | flops 134217728 | bytes 33652736
  128.1 29.4 %reduce-scatter.4.cloned.1.call-done = f32[1024,4]{1,0:T(8,128)} async-done(((f32[4096,4]{1,0:T(8,128)}), f32[1024,4]{1,0:T(8,128)}) %reduce-scatter.4.cloned.1.call-update) | async-done | bytes 16400
  157.5 1.8 %copy.35 = bf16[4,1024]{1,0:T(4,128)(2,1)} copy(f32[4,1024]{0,1:T(8,128)} %bitcast.79) | data formatting | bytes 24576
  (84 shorter events, 6.8 us)
Async XLA Ops:
  6.5 150.9 %reduce-scatter.4.cloned.1.call-start = ((), (), s32[]{:S(2)}) async-start(), calls=%async_computation.1 | async-start | bytes 2621440
  54.3 4.8 %collective-permute-start.3 = (f32[4,32,128]{2,1,0:T(8,128)S(1)}, f32[4,32,128]{2,1,0:T(8,128)S(1)}, u32[]{:S(2)}, u32[]{:S(2)}) collective-permute-start(f32[4,32,128]{2,1,0:T(8,128)S(1)} %fusion.37), channel_id=1, source_target_pairs={{0,1},{1,2},{2,3},{3,0},{4,5},{5,6},{6,7},{7,4},{8,9},{9,10},{10,1... | collective-permute-start | bytes 196616 | tf_op jit(solution)/shard_map/while/body/eval_jaxpr/ppermute | solution.py:19
  54.4 4.7 %collective-permute-start = (bf16[4,32,128]{2,1,0:T(8,128)(2,1)S(1)}, bf16[4,32,128]{2,1,0:T(8,128)(2,1)S(1)}, u32[]{:S(2)}, u32[]{:S(2)}) collective-permute-start(bf16[4,32,128]{2,1,0:T(8,128)(2,1)S(1)} %copy.76), channel_id=1, source_target_pairs={{0,1},{1,2},{2,3},{3,0},{4,5},{5,6},{6,7},{7,4},{8,9},{9,10},{10,1... | collective-permute-start | bytes 98312 | tf_op jit(solution)/shard_map/while/body/eval_jaxpr/ppermute | solution.py:19
  56.0 3.0 %collective-permute-start.1 = (f32[4,32]{1,0:T(4,128)S(1)}, f32[4,32]{1,0:T(4,128)S(1)}, u32[]{:S(2)}, u32[]{:S(2)}) collective-permute-start(f32[4,32]{1,0:T(4,128)S(1)} %get-tuple-element.343), channel_id=1, source_target_pairs={{0,1},{1,2},{2,3},{3,0},{4,5},{5,6},{6,7},{7,4},{8,9},{9,10},{10,1... | collective-permute-start | bytes 1544 | tf_op jit(solution)/shard_map/while/body/eval_jaxpr/ppermute | solution.py:19
  56.0 3.0 %collective-permute-start.2 = (f32[4,32]{1,0:T(4,128)S(1)}, f32[4,32]{1,0:T(4,128)S(1)}, u32[]{:S(2)}, u32[]{:S(2)}) collective-permute-start(f32[4,32]{1,0:T(4,128)S(1)} %get-tuple-element.344), channel_id=1, source_target_pairs={{0,1},{1,2},{2,3},{3,0},{4,5},{5,6},{6,7},{7,4},{8,9},{9,10},{10,1... | collective-permute-start | bytes 1544 | tf_op jit(solution)/shard_map/while/body/eval_jaxpr/ppermute | solution.py:19
  60.1 4.2 %collective-permute-start.3 = (f32[4,32,128]{2,1,0:T(8,128)S(1)}, f32[4,32,128]{2,1,0:T(8,128)S(1)}, u32[]{:S(2)}, u32[]{:S(2)}) collective-permute-start(f32[4,32,128]{2,1,0:T(8,128)S(1)} %fusion.37), channel_id=1, source_target_pairs={{0,1},{1,2},{2,3},{3,0},{4,5},{5,6},{6,7},{7,4},{8,9},{9,10},{10,1... | collective-permute-start | bytes 196616 | tf_op jit(solution)/shard_map/while/body/eval_jaxpr/ppermute | solution.py:19
  60.2 4.1 %collective-permute-start = (bf16[4,32,128]{2,1,0:T(8,128)(2,1)S(1)}, bf16[4,32,128]{2,1,0:T(8,128)(2,1)S(1)}, u32[]{:S(2)}, u32[]{:S(2)}) collective-permute-start(bf16[4,32,128]{2,1,0:T(8,128)(2,1)S(1)} %copy.76), channel_id=1, source_target_pairs={{0,1},{1,2},{2,3},{3,0},{4,5},{5,6},{6,7},{7,4},{8,9},{9,10},{10,1... | collective-permute-start | bytes 98312 | tf_op jit(solution)/shard_map/while/body/eval_jaxpr/ppermute | solution.py:19
  61.2 3.0 %collective-permute-start.1 = (f32[4,32]{1,0:T(4,128)S(1)}, f32[4,32]{1,0:T(4,128)S(1)}, u32[]{:S(2)}, u32[]{:S(2)}) collective-permute-start(f32[4,32]{1,0:T(4,128)S(1)} %get-tuple-element.343), channel_id=1, source_target_pairs={{0,1},{1,2},{2,3},{3,0},{4,5},{5,6},{6,7},{7,4},{8,9},{9,10},{10,1... | collective-permute-start | bytes 1544 | tf_op jit(solution)/shard_map/while/body/eval_jaxpr/ppermute | solution.py:19
  61.3 3.0 %collective-permute-start.2 = (f32[4,32]{1,0:T(4,128)S(1)}, f32[4,32]{1,0:T(4,128)S(1)}, u32[]{:S(2)}, u32[]{:S(2)}) collective-permute-start(f32[4,32]{1,0:T(4,128)S(1)} %get-tuple-element.344), channel_id=1, source_target_pairs={{0,1},{1,2},{2,3},{3,0},{4,5},{5,6},{6,7},{7,4},{8,9},{9,10},{10,1... | collective-permute-start | bytes 1544 | tf_op jit(solution)/shard_map/while/body/eval_jaxpr/ppermute | solution.py:19
  65.4 4.3 %collective-permute-start.3 = (f32[4,32,128]{2,1,0:T(8,128)S(1)}, f32[4,32,128]{2,1,0:T(8,128)S(1)}, u32[]{:S(2)}, u32[]{:S(2)}) collective-permute-start(f32[4,32,128]{2,1,0:T(8,128)S(1)} %fusion.37), channel_id=1, source_target_pairs={{0,1},{1,2},{2,3},{3,0},{4,5},{5,6},{6,7},{7,4},{8,9},{9,10},{10,1... | collective-permute-start | bytes 196616 | tf_op jit(solution)/shard_map/while/body/eval_jaxpr/ppermute | solution.py:19
  65.4 4.3 %collective-permute-start = (bf16[4,32,128]{2,1,0:T(8,128)(2,1)S(1)}, bf16[4,32,128]{2,1,0:T(8,128)(2,1)S(1)}, u32[]{:S(2)}, u32[]{:S(2)}) collective-permute-start(bf16[4,32,128]{2,1,0:T(8,128)(2,1)S(1)} %copy.76), channel_id=1, source_target_pairs={{0,1},{1,2},{2,3},{3,0},{4,5},{5,6},{6,7},{7,4},{8,9},{9,10},{10,1... | collective-permute-start | bytes 98312 | tf_op jit(solution)/shard_map/while/body/eval_jaxpr/ppermute | solution.py:19
  66.6 3.0 %collective-permute-start.1 = (f32[4,32]{1,0:T(4,128)S(1)}, f32[4,32]{1,0:T(4,128)S(1)}, u32[]{:S(2)}, u32[]{:S(2)}) collective-permute-start(f32[4,32]{1,0:T(4,128)S(1)} %get-tuple-element.343), channel_id=1, source_target_pairs={{0,1},{1,2},{2,3},{3,0},{4,5},{5,6},{6,7},{7,4},{8,9},{9,10},{10,1... | collective-permute-start | bytes 1544 | tf_op jit(solution)/shard_map/while/body/eval_jaxpr/ppermute | solution.py:19
  66.7 3.0 %collective-permute-start.2 = (f32[4,32]{1,0:T(4,128)S(1)}, f32[4,32]{1,0:T(4,128)S(1)}, u32[]{:S(2)}, u32[]{:S(2)}) collective-permute-start(f32[4,32]{1,0:T(4,128)S(1)} %get-tuple-element.344), channel_id=1, source_target_pairs={{0,1},{1,2},{2,3},{3,0},{4,5},{5,6},{6,7},{7,4},{8,9},{9,10},{10,1... | collective-permute-start | bytes 1544 | tf_op jit(solution)/shard_map/while/body/eval_jaxpr/ppermute | solution.py:19
  70.8 4.2 %collective-permute-start.3 = (f32[4,32,128]{2,1,0:T(8,128)S(1)}, f32[4,32,128]{2,1,0:T(8,128)S(1)}, u32[]{:S(2)}, u32[]{:S(2)}) collective-permute-start(f32[4,32,128]{2,1,0:T(8,128)S(1)} %fusion.37), channel_id=1, source_target_pairs={{0,1},{1,2},{2,3},{3,0},{4,5},{5,6},{6,7},{7,4},{8,9},{9,10},{10,1... | collective-permute-start | bytes 196616 | tf_op jit(solution)/shard_map/while/body/eval_jaxpr/ppermute | solution.py:19
  70.9 4.1 %collective-permute-start = (bf16[4,32,128]{2,1,0:T(8,128)(2,1)S(1)}, bf16[4,32,128]{2,1,0:T(8,128)(2,1)S(1)}, u32[]{:S(2)}, u32[]{:S(2)}) collective-permute-start(bf16[4,32,128]{2,1,0:T(8,128)(2,1)S(1)} %copy.76), channel_id=1, source_target_pairs={{0,1},{1,2},{2,3},{3,0},{4,5},{5,6},{6,7},{7,4},{8,9},{9,10},{10,1... | collective-permute-start | bytes 98312 | tf_op jit(solution)/shard_map/while/body/eval_jaxpr/ppermute | solution.py:19
  71.9 3.0 %collective-permute-start.1 = (f32[4,32]{1,0:T(4,128)S(1)}, f32[4,32]{1,0:T(4,128)S(1)}, u32[]{:S(2)}, u32[]{:S(2)}) collective-permute-start(f32[4,32]{1,0:T(4,128)S(1)} %get-tuple-element.343), channel_id=1, source_target_pairs={{0,1},{1,2},{2,3},{3,0},{4,5},{5,6},{6,7},{7,4},{8,9},{9,10},{10,1... | collective-permute-start | bytes 1544 | tf_op jit(solution)/shard_map/while/body/eval_jaxpr/ppermute | solution.py:19
  72.0 3.0 %collective-permute-start.2 = (f32[4,32]{1,0:T(4,128)S(1)}, f32[4,32]{1,0:T(4,128)S(1)}, u32[]{:S(2)}, u32[]{:S(2)}) collective-permute-start(f32[4,32]{1,0:T(4,128)S(1)} %get-tuple-element.344), channel_id=1, source_target_pairs={{0,1},{1,2},{2,3},{3,0},{4,5},{5,6},{6,7},{7,4},{8,9},{9,10},{10,1... | collective-permute-start | bytes 1544 | tf_op jit(solution)/shard_map/while/body/eval_jaxpr/ppermute | solution.py:19
Sparse Core Ops, SparseCore 0:
  128.2 29.2 reduce-scatter.3
where the time goes:
time: 167 us; the launch traced here: 166 us
  blocking collectives  74.3 us (44%)
  waiting for transfers between devices  37.6 us (23%)
  matrix products  20.5 us (12%)
  between operations  14.1 us (8%)
  starting transfers between devices  9.21 us (6%)
  local copies, waits for them, and re-layouts  7.76 us (5%)
  other arithmetic  2.39 us (1%)
    unnamed x2, waiting for transfers between devices  29.4 us
    unnamed x1, blocking collectives  19.6 us
    unnamed x1, matrix products  18.2 us
    all_gather x1, blocking collectives, per_device(): lax.all_gather(new_keys, 'beam', axis=0, tiled=True)  14.9 us
    all_gather x1, blocking collectives, per_device(): lax.all_gather(queries, 'beam', axis=0, tiled=True)  13.4 us
    all_gather x1, blocking collectives, per_device(): lax.all_gather(new_values, 'beam', axis=0, tiled=True)  13.3 us
    all_gather x1, blocking collectives, per_device(): all_beams = lax.all_gather(attended, 'beam', axis=0, tiled=True)  13.1 us
    ppermute x16, starting transfers between devices, shifted(): lax.ppermute(array, axis, [(i, (i + by) % length) for i in range(length)])  9.2 us
  transfers between devices with their start and end apart: 17, of which 9 were waited for; matrix products, arithmetic and copies ran while one was open for 0% of the time, Pallas kernels for 0%

commit v1 on v0

v1 whole, which is shorter than its diff:
```python
import functools
import math

import jax
import jax.numpy as jnp
from jax import lax
from jax.experimental import pallas as pl
from jax.experimental.pallas import tpu as pltpu
from jax.sharding import PartitionSpec as P

H = 128
KVH = 8
HD = 128
SPAN = 128
GROUP = H // KVH
MASKED = -1e30
LANES = 128
MESH = pl.DeviceIdType.MESH
F32 = jnp.float32
BF16 = jnp.bfloat16


def split3(x):
    hi = x.astype(BF16).astype(F32)
    mid = (x - hi).astype(BF16).astype(F32)
    return hi, mid, x - hi - mid


def kernel(
    nb, nc, hs, rows_total, tokens,
    q_hbm, nk_hbm, nv_hbm, ck_hbm, cv_hbm, par_hbm, len_hbm, w_hbm,
    out_ref,
    w_vm, ck_vm, cv_vm, k32, v32, kh, vh,
    q_in, nk_in, nv_in, par_sm, len_sm,
    q_rows, q_buf, n_buf, d_send, d_recv, e_buf, a_rows, g_send, g_recv,
    in_sem, w_sem, qs_sem, qr_sem, ns_sem, nr_sem, ds_sem, dr_sem,
    es_sem, er_sem, gs_sem, gr_sem,
):
    g = lax.axis_index("groups")
    p = lax.axis_index("beam")
    c = lax.axis_index("ctx")
    rp = max(hs, GROUP)
    units = rp // GROUP
    ur = nb * GROUP
    quarter = w_vm.shape[2]

    def dev(b, s):
        return (g, b, s)

    def cmod(k):
        return lax.rem(c + k, nc)

    def pmod(j):
        return lax.rem(p + j, nb)

    loads = []
    for i, (src, dst) in enumerate(
        (
            (q_hbm, q_in), (nk_hbm, nk_in), (nv_hbm, nv_in),
            (par_hbm, par_sm), (len_hbm, len_sm),
            (ck_hbm.at[0], ck_vm), (cv_hbm.at[0], cv_vm),
        )
    ):
        load = pltpu.make_async_copy(src, dst, in_sem.at[i])
        load.start()
        loads.append(load)

    def w_load(k):
        s = cmod(k)
        return pltpu.make_async_copy(
            w_hbm.at[:, pl.ds(pl.multiple_of(s * quarter, quarter), quarter)],
            w_vm.at[s],
            w_sem.at[k],
        )

    order = [k for k in range(1, nc)] + [0]
    for k in order:
        w_load(k).start()

    barrier = pltpu.get_barrier_semaphore()

    def greet(i, carry):
        b = pmod(i // nc)
        s = cmod(lax.rem(i, nc))
        pl.semaphore_signal(barrier, inc=1, device_id=dev(b, s), device_id_type=MESH)
        return carry

    lax.fori_loop(1, nb * nc, greet, 0)

    for i in range(3):
        loads[i].wait()
    q_rows[...] = jnp.zeros_like(q_rows)
    q_flat = q_in[...].astype(F32)
    for h in range(hs):
        q_rows[h : h + 1, :] = q_flat[:, h * HD : (h + 1) * HD]
    q_buf[c, p] = q_rows[...].astype(BF16)
    kv0 = (c * hs) // GROUP
    row16 = lax.broadcasted_iota(jnp.int32, (16, HD), 0)
    staged = jnp.zeros((16, HD), F32)
    for u in range(units):
        lane0 = pl.multiple_of((kv0 + u) * HD, HD)
        staged = jnp.where(row16 == u, nk_in[:, pl.ds(lane0, HD)].astype(F32), staged)
        staged = jnp.where(row16 == 8 + u, nv_in[:, pl.ds(lane0, HD)].astype(F32), staged)
    n_buf[p] = staged.astype(BF16)

    pl.semaphore_wait(barrier, nb * nc - 1)

    def q_copy(j, k):
        return pltpu.make_async_remote_copy(
            src_ref=q_buf.at[c, p],
            dst_ref=q_buf.at[c, p],
            send_sem=qs_sem.at[j, k],
            recv_sem=qr_sem.at[c, p],
            device_id=dev(pmod(j), cmod(k)),
            device_id_type=MESH,
        )

    def n_copy(j):
        return pltpu.make_async_remote_copy(
            src_ref=n_buf.at[p],
            dst_ref=n_buf.at[p],
            send_sem=ns_sem.at[j],
            recv_sem=nr_sem.at[p],
            device_id=dev(pmod(j), c),
            device_id_type=MESH,
        )

    def q_arrival(b, s):
        return pltpu.make_async_remote_copy(
            src_ref=q_buf.at[s, b],
            dst_ref=q_buf.at[s, b],
            send_sem=qs_sem.at[0, 0],
            recv_sem=qr_sem.at[s, b],
            device_id=dev(pmod(1), c),
            device_id_type=MESH,
        )

    for k in range(nc - 1, -1, -1):
        for j in range(nb - 1, -1, -1):
            if j or k:
                q_copy(j, k).start()
    for j in range(nb - 1, 0, -1):
        n_copy(j).start()

    loads[5].wait()
    step = 64

    def widen(src, dst):
        def body(i, carry):
            t0 = pl.multiple_of(i * step, step)
            block = src[pl.ds(t0, step)].astype(F32)
            dst[pl.ds(pl.multiple_of(t0 * KVH, step * KVH), step * KVH), :] = block.reshape(
                step * KVH, HD
            )
            return carry

        lax.fori_loop(0, tokens // step, body, 0)

    widen(ck_vm, k32)
    for kv in range(KVH):
        kh[kv] = k32[pl.ds(kv, tokens, stride=KVH), :].astype(BF16)
    loads[6].wait()
    widen(cv_vm, v32)
    for kv in range(KVH):
        vh[kv] = v32[pl.ds(kv, tokens, stride=KVH), :].astype(BF16)
    loads[3].wait()
    loads[4].wait()
    limit = len_sm[p] * SPAN
    position = c * tokens + lax.broadcasted_iota(jnp.int32, (ur, tokens), 1)
    usable = position < limit
    scale = 1.0 / math.sqrt(HD)
    lane_u = lax.broadcasted_iota(jnp.int32, (ur, LANES), 1)
    row_u = lax.broadcasted_iota(jnp.int32, (ur, LANES), 0)
    row16 = lax.broadcasted_iota(jnp.int32, (16, LANES), 0)

    def to_lanes(column, u):
        return jnp.sum(jnp.where(lane_u == row_u + u * ur, column, 0.0), axis=0, keepdims=True)

    def attend(s):
        kv_base = (s * hs) // GROUP
        peak_row = jnp.zeros((1, LANES), F32)
        sum_row = jnp.zeros((1, LANES), F32)
        for u in range(units):
            q = jnp.concatenate(
                [q_buf[s, b, u * GROUP : (u + 1) * GROUP, :] for b in range(nb)], axis=0
            )
            scores = lax.dot_general(
                q, kh[kv_base + u], (((1,), (1,)), ((), ())), preferred_element_type=F32
            )
            scores = jnp.where(usable, scores * scale, MASKED)
            peak = jnp.max(scores, axis=1, keepdims=True)
            weights = jnp.where(usable, jnp.exp(scores - peak), 0.0)
            total = jnp.sum(weights, axis=1, keepdims=True)
            blended = jnp.dot(weights.astype(BF16), vh[kv_base + u], preferred_element_type=F32)
            d_send[s, u * ur : (u + 1) * ur, :] = blended.astype(BF16)
            peak_row = peak_row + to_lanes(peak, u)
            sum_row = sum_row + to_lanes(total, u)
        stats = jnp.zeros((16, LANES), F32)
        for i, piece in enumerate(split3(peak_row) + split3(sum_row)):
            stats = jnp.where(row16 == i, piece, stats)
        d_send[s, units * ur : units * ur + 16, :] = stats.astype(BF16)

    def d_copy(k):
        return pltpu.make_async_remote_copy(
            src_ref=d_send.at[cmod(k)],
            dst_ref=d_recv.at[c],
            send_sem=ds_sem.at[k],
            recv_sem=dr_sem.at[c],
            device_id=dev(p, cmod(k)),
            device_id_type=MESH,
        )

    def d_arrival(s):
        return pltpu.make_async_remote_copy(
            src_ref=d_recv.at[s],
            dst_ref=d_recv.at[s],
            send_sem=ds_sem.at[0],
            recv_sem=dr_sem.at[s],
            device_id=dev(p, cmod(1)),
            device_id_type=MESH,
        )

    for k in order:
        s = cmod(k)
        for j in range(nb):
            if j or k:
                q_arrival(pmod(j), s).wait_recv()
        attend(s)
        if k:
            d_copy(k).start()

    for j in range(1, nb):
        pltpu.make_async_remote_copy(
            src_ref=n_buf.at[pmod(j)],
            dst_ref=n_buf.at[pmod(j)],
            send_sem=ns_sem.at[0],
            recv_sem=nr_sem.at[pmod(j)],
            device_id=dev(pmod(j), c),
            device_id_type=MESH,
        ).wait_recv()
    own_row = jnp.zeros((1, LANES), F32)
    own_values = []
    for u in range(units):
        own_scores = []
        for b in range(nb):
            fresh = n_buf[b].astype(F32)
            q = q_buf[c, b, u * GROUP : (u + 1) * GROUP, :].astype(F32)
            own_scores.append(jnp.sum(q * fresh[u : u + 1], axis=1, keepdims=True))
            own_values.append(jnp.broadcast_to(fresh[8 + u : 9 + u], (GROUP, HD)))
        own_row = own_row + to_lanes(
            jnp.broadcast_to(jnp.concatenate(own_scores, axis=0), (ur, LANES)), u
        )
    own_row = own_row * scale
    own_value = jnp.concatenate(own_values, axis=0)

    for k in range(1, nc):
        d_arrival(cmod(k)).wait_recv()
    rows = units * ur
    states = []
    for k in range(nc):
        ref = d_send if k == 0 else d_recv
        s = cmod(k)
        stats = ref[s, rows : rows + 16, :].astype(F32)
        states.append(
            (
                ref, s,
                stats[0:1] + stats[1:2] + stats[2:3],
                stats[3:4] + stats[4:5] + stats[5:6],
            )
        )
    top = own_row
    for _, _, peak, _ in states:
        top = jnp.maximum(top, peak)
    own_scale = jnp.exp(own_row - top)
    total = own_scale
    scales = []
    for _, _, peak, weight_sum in states:
        factor = jnp.exp(peak - top)
        scales.append(factor)
        total = total + weight_sum * factor
    inverse = 1.0 / total
    lane_r = lax.broadcasted_iota(jnp.int32, (rows, LANES), 1)
    row_r = lax.broadcasted_iota(jnp.int32, (rows, LANES), 0)
    diagonal = lane_r == row_r

    def to_rows(lanes):
        return jnp.sum(jnp.where(diagonal, lanes, 0.0), axis=1, keepdims=True)

    result = own_value * to_rows(own_scale * inverse)
    for (ref, s, _, _), factor in zip(states, scales):
        result = result + ref[s, 0:rows, :].astype(F32) * to_rows(factor * inverse)
    e_buf[p] = result.astype(BF16)

    def e_copy(j):
        return pltpu.make_async_remote_copy(
            src_ref=e_buf.at[p],
            dst_ref=e_buf.at[p],
            send_sem=es_sem.at[j],
            recv_sem=er_sem.at[p],
            device_id=dev(pmod(j), c),
            device_id_type=MESH,
        )

    for j in range(nb - 1, 0, -1):
        e_copy(j).start()
    for j in range(1, nb):
        pltpu.make_async_remote_copy(
            src_ref=e_buf.at[pmod(j)],
            dst_ref=e_buf.at[pmod(j)],
            send_sem=es_sem.at[0],
            recv_sem=er_sem.at[pmod(j)],
            device_id=dev(pmod(j), c),
            device_id_type=MESH,
        ).wait_recv()
    for b in range(nb):
        parent = par_sm[b]
        for u in range(units):
            r0 = u * ur + b * GROUP
            a_rows[r0 : r0 + GROUP, :] = e_buf[parent, r0 : r0 + GROUP, :].astype(F32)
    heads = []
    for h in range(hs):
        r0 = (h // GROUP) * ur + h % GROUP
        heads.append(a_rows[pl.ds(r0, nb, stride=GROUP), :])
    attended = jnp.concatenate(heads, axis=1).astype(BF16)

    def g_copy(k):
        return pltpu.make_async_remote_copy(
            src_ref=g_send.at[cmod(k)],
            dst_ref=g_recv.at[c],
            send_sem=gs_sem.at[k],
            recv_sem=gr_sem.at[c],
            device_id=dev(p, cmod(k)),
            device_id_type=MESH,
        )

    chunk = min(512, quarter)
    for k in order:
        s = cmod(k)
        w_load(k).wait()

        def multiply(i, carry):
            n0 = pl.multiple_of(i * chunk, chunk)
            g_send[s, :, pl.ds(n0, chunk)] = jnp.dot(
                attended, w_vm[s, :, pl.ds(n0, chunk)], preferred_element_type=F32
            )
            return carry

        lax.fori_loop(0, quarter // chunk, multiply, 0)
        if k:
            g_copy(k).start()
    total_out = g_send[c]
    for k in range(1, nc):
        s = cmod(k)
        pltpu.make_async_remote_copy(
            src_ref=g_recv.at[s],
            dst_ref=g_recv.at[s],
            send_sem=gs_sem.at[0],
            recv_sem=gr_sem.at[s],
            device_id=dev(p, cmod(1)),
            device_id_type=MESH,
        ).wait_recv()
        total_out = total_out + g_recv[s]
    out_ref[...] = total_out.astype(BF16)

    for k in range(nc):
        for j in range(nb):
            if j or k:
                q_copy(j, k).wait_send()
    for j in range(1, nb):
        n_copy(j).wait_send()
        e_copy(j).wait_send()
    for k in range(1, nc):
        d_copy(k).wait_send()
        g_copy(k).wait_send()


def per_device(nb, nc, queries, new_keys, new_values, cache_keys, cache_values, parents, lengths, out_weight):
    hs = queries.shape[1] // HD
    tokens = cache_keys.shape[1]
    rp = max(hs, GROUP)
    rows = (rp // GROUP) * nb * GROUP
    depth, columns = out_weight.shape
    quarter = columns // nc
    dma = pltpu.SemaphoreType.DMA
    return pl.pallas_call(
        functools.partial(kernel, nb, nc, hs, rows, tokens),
        out_shape=jax.ShapeDtypeStruct((nb, quarter), BF16),
        in_specs=[pl.BlockSpec(memory_space=pl.ANY)] * 8,
        out_specs=pl.BlockSpec(memory_space=pltpu.VMEM),
        scratch_shapes=[
            pltpu.VMEM((nc, depth, quarter), BF16),
            pltpu.VMEM((tokens, KVH, HD), BF16),
            pltpu.VMEM((tokens, KVH, HD), BF16),
            pltpu.VMEM((tokens * KVH, HD), F32),
            pltpu.VMEM((tokens * KVH, HD), F32),
            pltpu.VMEM((KVH, tokens, HD), BF16),
            pltpu.VMEM((KVH, tokens, HD), BF16),
            pltpu.VMEM(queries.shape, BF16),
            pltpu.VMEM(new_keys.shape, BF16),
            pltpu.VMEM(new_values.shape, BF16),
            pltpu.SMEM(parents.shape, jnp.int32),
            pltpu.SMEM(lengths.shape, jnp.int32),
            pltpu.VMEM((rp, HD), F32),
            pltpu.VMEM((nc, nb, rp, HD), BF16),
            pltpu.VMEM((nb, 16, HD), BF16),
            pltpu.VMEM((nc, rows + 16, HD), BF16),
            pltpu.VMEM((nc, rows + 16, HD), BF16),
            pltpu.VMEM((nb, rows, HD), BF16),
            pltpu.VMEM((rows, HD), F32),
            pltpu.VMEM((nc, nb, quarter), F32),
            pltpu.VMEM((nc, nb, quarter), F32),
            dma((7,)),
            dma((nc,)),
            dma((nb, nc)),
            dma((nc, nb)),
            dma((nb,)),
            dma((nb,)),
            dma((nc,)),
            dma((nc,)),
            dma((nb,)),
            dma((nb,)),
            dma((nc,)),
            dma((nc,)),
        ],
        compiler_params=pltpu.CompilerParams(
            collective_id=0, has_side_effects=True, vmem_limit_bytes=60 * 1024 * 1024
        ),
    )(queries, new_keys, new_values, cache_keys, cache_values, parents, lengths, out_weight)


def solution(mesh):
    placed = (
        P(("groups", "beam"), "ctx"),
        P(("groups", "beam"), None),
        P(("groups", "beam"), None),
        P(("groups", "beam"), "ctx", None, None),
        P(("groups", "beam"), "ctx", None, None),
        P("groups"),
        P("groups"),
        P("ctx", "beam"),
    )
    return jax.shard_map(
        functools.partial(per_device, mesh.shape["beam"], mesh.shape["ctx"]),
        mesh=mesh,
        in_specs=placed,
        out_specs=P("groups", ("beam", "ctx")),
        check_vma=False,
    )
```

time: 167 us -> 28.9 us (0.17)
  blocking collectives: 74.3 us -> 0 us
  waiting for transfers between devices: 37.6 us -> 0 us
  Pallas kernels: 0 us -> 27.2 us
  matrix products: 20.5 us -> 0 us
  between operations: 14.1 us -> 0.01 us
  starting transfers between devices: 9.21 us -> 0 us
  local copies, waits for them, and re-layouts: 7.76 us -> 1.3 us
  other arithmetic: 2.39 us -> 0 us
    all_gather x4 -> x0, blocking collectives: 54.7 us -> none  [the longest x1 14.9 us: per_device(): lax.all_gather(new_keys, 'beam', axis=0, tiled=True)]
    unnamed x2 -> x0, waiting for transfers between devices: 29.4 us -> none
    pallas_call x0 -> x1, Pallas kernels: none -> 27.2 us  [per_device(): pl.pallas_call(functools.partial(kernel, nb, nc, hs, rows, tokens), out_s...]
    unnamed x1 -> x0, blocking collectives: 19.6 us -> none
    unnamed x1 -> x0, matrix products: 18.2 us -> none
    ppermute x16 -> x0, starting transfers between devices: 9.2 us -> none  [shifted(): lax.ppermute(array, axis, [(i, (i + by) % length) for i in range(length)])]
    ppermute x16 -> x0, waiting for transfers between devices: 8.23 us -> none  [shifted(): lax.ppermute(array, axis, [(i, (i + by) % length) for i in range(length)])]
    unnamed x6 -> x1, local copies, waits for them, and re-layouts: 3.76 us -> 1.3 us
  transfers between devices with their start and end apart: 17 -> 0, of which waited for: 9 -> 0; matrix products, arithmetic and copies ran while one was open for 0% -> 0% of each run, Pallas kernels for 0% -> 0%
where the time goes in v1:
time: 28.9 us; the launch traced here: 28.5 us
  Pallas kernels  27.2 us (94%)
  local copies, waits for them, and re-layouts  1.3 us (4%)
    pallas_call x1, Pallas kernels, per_device(): pl.pallas_call(functools.partial(kernel, nb, nc, hs, rows, tokens), out_s...  27.2 us
    unnamed x1, local copies, waits for them, and re-layouts  1.3 us

profile of v1, /device:TPU:0, one launch (start us, length us, event | category | flops | bytes accessed | tf_op | source)
XLA Modules:
  0.0 28.5 jit_solution(1134787160637575487)
XLA Ops:
  0.0 27.2 %shard_map.82 = bf16[4,1024]{1,0:T(4,128)(2,1)} custom-call(bf16[1,4096]{1,0:T(2,128)(2,1)} %q_hbm.1, bf16[1,1024]{1,0:T(2,128)(2,1)} %nk_hbm.1, bf16[1,1024]{1,0:T(2,128)(2,1)} %nv_hbm.1, bf16[1,512,8,128]{3,2,1,0:T(8,128)(2,1)} %ck_hbm.1, bf16[1,512,8,128]{3,2,1,0:T(8,128)(2,1)} %cv_hbm.1, s32[4]{0:T(128)} %par_hbm.1, s32[4]{0:T(128)} %len_hbm.1, ...), custom_call_target="tpu_custom_call" | custom-call | tf_op jit(solution)/shard_map/pallas_call | solution.py:385
  27.2 1.3 %copy.10 = bf16[4,1024]{1,0:T(4,128)(2,1)} copy(bf16[4,1024]{1,0:T(4,128)(2,1)} %shard_map.82) | data formatting | bytes 16384

commit v2 on v1

v2 whole, which is shorter than its diff:
```python
import functools
import math

import jax
import jax.numpy as jnp
from jax import lax
from jax.experimental import pallas as pl
from jax.experimental.pallas import tpu as pltpu
from jax.sharding import PartitionSpec as P

H = 128
KVH = 8
HD = 128
SPAN = 128
GROUP = H // KVH
LOWEST = -3.0e38
LANES = 128
MESH = pl.DeviceIdType.MESH
F32 = jnp.float32
BF16 = jnp.bfloat16


def split3(x):
    hi = x.astype(BF16).astype(F32)
    mid = (x - hi).astype(BF16).astype(F32)
    return hi, mid, x - hi - mid


def kernel(
    nb, nc, hs, tokens,
    q_hbm, nk_hbm, nv_hbm, ck_hbm, cv_hbm, par_hbm, len_hbm, w_hbm,
    out_ref,
    w_vm, ck_vm, cv_vm, k32, v32, kh, vh,
    q_in, nk_in, nv_in, par_sm, len_sm,
    q_rows, q_buf, n_buf, d_send, d_recv, e_buf, a_rows, g_send, g_recv,
    in_sem, w_sem, qs_sem, qr_sem, ns_sem, nr_sem, ds_sem, dr_sem,
    es_sem, er_sem, gs_sem, gr_sem,
):
    g = lax.axis_index("groups")
    p = lax.axis_index("beam")
    c = lax.axis_index("ctx")
    rp = max(hs, GROUP)
    units = rp // GROUP
    ur = nb * GROUP
    quarter = w_vm.shape[2]

    def dev(b, s):
        return (g, b, s)

    def cmod(k):
        return lax.rem(c + k, nc)

    def pmod(j):
        return lax.rem(p + j, nb)

    loads = []
    for i, (src, dst) in enumerate(
        (
            (q_hbm, q_in), (nk_hbm, nk_in), (nv_hbm, nv_in),
            (par_hbm, par_sm), (len_hbm, len_sm),
            (ck_hbm.at[0], ck_vm), (cv_hbm.at[0], cv_vm),
        )
    ):
        load = pltpu.make_async_copy(src, dst, in_sem.at[i])
        load.start()
        loads.append(load)

    part = w_vm.shape[1] // units

    def w_load(u, k):
        s = cmod(k)
        return pltpu.make_async_copy(
            w_hbm.at[
                u * part : (u + 1) * part,
                pl.ds(pl.multiple_of(s * quarter, quarter), quarter),
            ],
            w_vm.at[s, u * part : (u + 1) * part],
            w_sem.at[u, k],
        )

    order = [k for k in range(1, nc)] + [0]
    for u in range(units):
        for k in order:
            w_load(u, k).start()

    barrier = pltpu.get_barrier_semaphore()

    def greet(i, carry):
        b = pmod(i // nc)
        s = cmod(lax.rem(i, nc))
        pl.semaphore_signal(barrier, inc=1, device_id=dev(b, s), device_id_type=MESH)
        return carry

    lax.fori_loop(1, nb * nc, greet, 0)

    for i in range(3):
        loads[i].wait()
    q_rows[...] = jnp.zeros_like(q_rows)
    q_flat = q_in[...].astype(F32)
    for h in range(hs):
        q_rows[h : h + 1, :] = q_flat[:, h * HD : (h + 1) * HD]
    q_buf[c, p] = q_rows[...].astype(BF16)
    kv0 = (c * hs) // GROUP
    row16 = lax.broadcasted_iota(jnp.int32, (16, HD), 0)
    staged = jnp.zeros((16, HD), F32)
    for u in range(units):
        lane0 = pl.multiple_of((kv0 + u) * HD, HD)
        staged = jnp.where(row16 == u, nk_in[:, pl.ds(lane0, HD)].astype(F32), staged)
        staged = jnp.where(row16 == 8 + u, nv_in[:, pl.ds(lane0, HD)].astype(F32), staged)
    n_buf[p] = staged.astype(BF16)

    pl.semaphore_wait(barrier, nb * nc - 1)

    def q_copy(j, k):
        return pltpu.make_async_remote_copy(
            src_ref=q_buf.at[c, p],
            dst_ref=q_buf.at[c, p],
            send_sem=qs_sem.at[j, k],
            recv_sem=qr_sem.at[c, p],
            device_id=dev(pmod(j), cmod(k)),
            device_id_type=MESH,
        )

    def n_copy(j):
        return pltpu.make_async_remote_copy(
            src_ref=n_buf.at[p],
            dst_ref=n_buf.at[p],
            send_sem=ns_sem.at[j],
            recv_sem=nr_sem.at[p],
            device_id=dev(pmod(j), c),
            device_id_type=MESH,
        )

    def q_arrival(b, s):
        return pltpu.make_async_remote_copy(
            src_ref=q_buf.at[s, b],
            dst_ref=q_buf.at[s, b],
            send_sem=qs_sem.at[0, 0],
            recv_sem=qr_sem.at[s, b],
            device_id=dev(pmod(1), c),
            device_id_type=MESH,
        )

    for k in range(nc - 1, -1, -1):
        for j in range(nb - 1, -1, -1):
            if j or k:
                q_copy(j, k).start()
    for j in range(nb - 1, 0, -1):
        n_copy(j).start()

    loads[5].wait()
    step = 64

    def widen(src, dst):
        def body(i, carry):
            t0 = pl.multiple_of(i * step, step)
            block = src[pl.ds(t0, step)].astype(F32)
            dst[pl.ds(pl.multiple_of(t0 * KVH, step * KVH), step * KVH), :] = block.reshape(
                step * KVH, HD
            )
            return carry

        lax.fori_loop(0, tokens // step, body, 0)

    def extract(u):
        for kv in range(u, KVH, units):
            kh[kv] = k32[pl.ds(kv, tokens, stride=KVH), :].astype(BF16)
        for kv in range(u, KVH, units):
            vh[kv] = v32[pl.ds(kv, tokens, stride=KVH), :].astype(BF16)

    widen(ck_vm, k32)
    loads[6].wait()
    widen(cv_vm, v32)
    extract(0)
    loads[3].wait()
    loads[4].wait()
    limit = len_sm[p] * SPAN
    position = c * tokens + lax.broadcasted_iota(jnp.int32, (ur, tokens), 1)
    usable = position < limit
    scale = 1.0 / math.sqrt(HD)
    lane_u = lax.broadcasted_iota(jnp.int32, (ur, LANES), 1)
    row_u = lax.broadcasted_iota(jnp.int32, (ur, LANES), 0)
    row16 = lax.broadcasted_iota(jnp.int32, (16, LANES), 0)

    def to_lanes(column):
        return jnp.sum(jnp.where(lane_u == row_u, column, 0.0), axis=0, keepdims=True)

    def attend(s, u):
        kv = (s * hs) // GROUP + u
        q = jnp.concatenate(
            [q_buf[s, b, u * GROUP : (u + 1) * GROUP, :] for b in range(nb)], axis=0
        )
        scores = lax.dot_general(
            q, kh[kv], (((1,), (1,)), ((), ())), preferred_element_type=F32
        )
        scores = jnp.where(usable, scores * scale, -jnp.inf)
        peak = jnp.maximum(jnp.max(scores, axis=1, keepdims=True), LOWEST)
        weights = jnp.exp(scores - peak)
        total = jnp.sum(weights, axis=1, keepdims=True)
        blended = jnp.dot(weights.astype(BF16), vh[kv], preferred_element_type=F32)
        d_send[u, s, 0:ur, :] = blended.astype(BF16)
        stats = jnp.zeros((16, LANES), F32)
        for i, piece in enumerate(split3(to_lanes(peak)) + split3(to_lanes(total))):
            stats = jnp.where(row16 == i, piece, stats)
        d_send[u, s, ur : ur + 16, :] = stats.astype(BF16)

    def d_copy(u, k):
        return pltpu.make_async_remote_copy(
            src_ref=d_send.at[u, cmod(k)],
            dst_ref=d_recv.at[u, c],
            send_sem=ds_sem.at[u, k],
            recv_sem=dr_sem.at[u, c],
            device_id=dev(p, cmod(k)),
            device_id_type=MESH,
        )

    def d_arrival(u, s):
        return pltpu.make_async_remote_copy(
            src_ref=d_recv.at[u, s],
            dst_ref=d_recv.at[u, s],
            send_sem=ds_sem.at[u, 0],
            recv_sem=dr_sem.at[u, s],
            device_id=dev(p, cmod(1)),
            device_id_type=MESH,
        )

    for k in order:
        for j in range(nb):
            if j or k:
                q_arrival(pmod(j), cmod(k)).wait_recv()
    for u in range(units):
        if u:
            extract(u)
        for k in order:
            attend(cmod(k), u)
        for k in range(1, nc):
            d_copy(u, k).start()

    for j in range(1, nb):
        pltpu.make_async_remote_copy(
            src_ref=n_buf.at[pmod(j)],
            dst_ref=n_buf.at[pmod(j)],
            send_sem=ns_sem.at[0],
            recv_sem=nr_sem.at[pmod(j)],
            device_id=dev(pmod(j), c),
            device_id_type=MESH,
        ).wait_recv()
    own_rows = []
    own_values = []
    for u in range(units):
        own_scores = []
        unit_values = []
        for b in range(nb):
            fresh = n_buf[b].astype(F32)
            q = q_buf[c, b, u * GROUP : (u + 1) * GROUP, :].astype(F32)
            own_scores.append(jnp.sum(q * fresh[u : u + 1], axis=1, keepdims=True))
            unit_values.append(jnp.broadcast_to(fresh[8 + u : 9 + u], (GROUP, HD)))
        own_rows.append(to_lanes(jnp.concatenate(own_scores, axis=0)) * scale)
        own_values.append(jnp.concatenate(unit_values, axis=0))

    def to_rows(lanes):
        return jnp.sum(jnp.where(lane_u == row_u, lanes, 0.0), axis=1, keepdims=True)

    def combine(u):
        for k in range(1, nc):
            d_arrival(u, cmod(k)).wait_recv()
        states = []
        for k in range(nc):
            ref = d_send if k == 0 else d_recv
            s = cmod(k)
            stats = ref[u, s, ur : ur + 16, :].astype(F32)
            states.append(
                (
                    ref[u, s, 0:ur, :].astype(F32),
                    stats[0:1] + stats[1:2] + stats[2:3],
                    stats[3:4] + stats[4:5] + stats[5:6],
                )
            )
        top = own_rows[u]
        for _, peak, _ in states:
            top = jnp.maximum(top, peak)
        own_scale = jnp.exp(own_rows[u] - top)
        total = own_scale
        scales = []
        for _, peak, weight_sum in states:
            factor = jnp.exp(peak - top)
            scales.append(factor)
            total = total + weight_sum * factor
        inverse = 1.0 / total
        result = own_values[u] * to_rows(own_scale * inverse)
        for (blended, _, _), factor in zip(states, scales):
            result = result + blended * to_rows(factor * inverse)
        e_buf[u, p] = result.astype(BF16)

    def e_copy(u, j):
        return pltpu.make_async_remote_copy(
            src_ref=e_buf.at[u, p],
            dst_ref=e_buf.at[u, p],
            send_sem=es_sem.at[u, j],
            recv_sem=er_sem.at[u, p],
            device_id=dev(pmod(j), c),
            device_id_type=MESH,
        )

    def e_arrival(u, j):
        return pltpu.make_async_remote_copy(
            src_ref=e_buf.at[u, pmod(j)],
            dst_ref=e_buf.at[u, pmod(j)],
            send_sem=es_sem.at[u, 0],
            recv_sem=er_sem.at[u, pmod(j)],
            device_id=dev(pmod(j), c),
            device_id_type=MESH,
        )

    for u in range(units):
        combine(u)
        for j in range(nb - 1, 0, -1):
            e_copy(u, j).start()

    unit_heads = hs // units

    def gather_attended(u):
        for j in range(1, nb):
            e_arrival(u, j).wait_recv()
        for b in range(nb):
            r0 = b * GROUP
            chosen = e_buf[u, 0, r0 : r0 + GROUP, :].astype(F32)
            for j in range(1, nb):
                other = e_buf[u, j, r0 : r0 + GROUP, :].astype(F32)
                chosen = jnp.where(par_sm[b] == j, other, chosen)
            a_rows[u, r0 : r0 + GROUP, :] = chosen
        heads = [a_rows[u, pl.ds(h, nb, stride=GROUP), :] for h in range(unit_heads)]
        return jnp.concatenate(heads, axis=1).astype(BF16)

    def g_copy(k):
        return pltpu.make_async_remote_copy(
            src_ref=g_send.at[cmod(k)],
            dst_ref=g_recv.at[c],
            send_sem=gs_sem.at[k],
            recv_sem=gr_sem.at[c],
            device_id=dev(p, cmod(k)),
            device_id_type=MESH,
        )

    chunk = min(512, quarter)
    for u in range(units):
        attended = gather_attended(u)
        for k in order:
            s = cmod(k)
            w_load(u, k).wait()

            def multiply(i, carry):
                n0 = pl.multiple_of(i * chunk, chunk)
                product = jnp.dot(
                    attended,
                    w_vm[s, u * part : (u + 1) * part, pl.ds(n0, chunk)],
                    preferred_element_type=F32,
                )
                if u:
                    product = product + g_send[s, :, pl.ds(n0, chunk)]
                g_send[s, :, pl.ds(n0, chunk)] = product
                return carry

            lax.fori_loop(0, quarter // chunk, multiply, 0)
            if k and u == units - 1:
                g_copy(k).start()
    total_out = g_send[c]
    for k in range(1, nc):
        s = cmod(k)
        pltpu.make_async_remote_copy(
            src_ref=g_recv.at[s],
            dst_ref=g_recv.at[s],
            send_sem=gs_sem.at[0],
            recv_sem=gr_sem.at[s],
            device_id=dev(p, cmod(1)),
            device_id_type=MESH,
        ).wait_recv()
        total_out = total_out + g_recv[s]
    out_ref[...] = total_out.astype(BF16)

    for k in range(nc):
        for j in range(nb):
            if j or k:
                q_copy(j, k).wait_send()
    for j in range(1, nb):
        n_copy(j).wait_send()
    for u in range(units):
        for j in range(1, nb):
            e_copy(u, j).wait_send()
        for k in range(1, nc):
            d_copy(u, k).wait_send()
    for k in range(1, nc):
        g_copy(k).wait_send()


def per_device(nb, nc, queries, new_keys, new_values, cache_keys, cache_values, parents, lengths, out_weight):
    hs = queries.shape[1] // HD
    tokens = cache_keys.shape[1]
    rp = max(hs, GROUP)
    units = rp // GROUP
    ur = nb * GROUP
    depth, columns = out_weight.shape
    quarter = columns // nc
    dma = pltpu.SemaphoreType.DMA
    return pl.pallas_call(
        functools.partial(kernel, nb, nc, hs, tokens),
        out_shape=pltpu.VMEM((nb, quarter), BF16),
        in_specs=[pl.BlockSpec(memory_space=pltpu.HBM)] * 8,
        out_specs=pl.BlockSpec(memory_space=pltpu.VMEM),
        scratch_shapes=[
            pltpu.VMEM((nc, depth, quarter), BF16),
            pltpu.VMEM((tokens, KVH, HD), BF16),
            pltpu.VMEM((tokens, KVH, HD), BF16),
            pltpu.VMEM((tokens * KVH, HD), F32),
            pltpu.VMEM((tokens * KVH, HD), F32),
            pltpu.VMEM((KVH, tokens, HD), BF16),
            pltpu.VMEM((KVH, tokens, HD), BF16),
            pltpu.VMEM(queries.shape, BF16),
            pltpu.VMEM(new_keys.shape, BF16),
            pltpu.VMEM(new_values.shape, BF16),
            pltpu.SMEM(parents.shape, jnp.int32),
            pltpu.SMEM(lengths.shape, jnp.int32),
            pltpu.VMEM((rp, HD), F32),
            pltpu.VMEM((nc, nb, rp, HD), BF16),
            pltpu.VMEM((nb, 16, HD), BF16),
            pltpu.VMEM((units, nc, ur + 16, HD), BF16),
            pltpu.VMEM((units, nc, ur + 16, HD), BF16),
            pltpu.VMEM((units, nb, ur, HD), BF16),
            pltpu.VMEM((units, ur, HD), F32),
            pltpu.VMEM((nc, nb, quarter), F32),
            pltpu.VMEM((nc, nb, quarter), F32),
            dma((7,)),
            dma((units, nc)),
            dma((nb, nc)),
            dma((nc, nb)),
            dma((nb,)),
            dma((nb,)),
            dma((units, nc)),
            dma((units, nc)),
            dma((units, nb)),
            dma((units, nb)),
            dma((nc,)),
            dma((nc,)),
        ],
        compiler_params=pltpu.CompilerParams(
            collective_id=0, has_side_effects=True, vmem_limit_bytes=60 * 1024 * 1024
        ),
    )(queries, new_keys, new_values, cache_keys, cache_values, parents, lengths, out_weight)


def solution(mesh):
    placed = (
        P(("groups", "beam"), "ctx"),
        P(("groups", "beam"), None),
        P(("groups", "beam"), None),
        P(("groups", "beam"), "ctx", None, None),
        P(("groups", "beam"), "ctx", None, None),
        P("groups"),
        P("groups"),
        P("ctx", "beam"),
    )
    return jax.shard_map(
        functools.partial(per_device, mesh.shape["beam"], mesh.shape["ctx"]),
        mesh=mesh,
        in_specs=placed,
        out_specs=P("groups", ("beam", "ctx")),
        check_vma=False,
    )
```

time: 28.9 us -> 31.3 us (1.083)
  Pallas kernels: 27.2 us -> 30.4 us
  local copies, waits for them, and re-layouts: 1.3 us -> 0.6 us
    pallas_call x1, Pallas kernels: 27.2 us -> 30.4 us  [per_device(): pl.pallas_call(functools.partial(kernel, nb, nc, hs, tokens), out_shape=p...]
    unnamed x1, local copies, waits for them, and re-layouts: 1.3 us -> 0.6 us
where the time goes in v2:
time: 31.3 us; the launch traced here: 31 us
  Pallas kernels  30.4 us (97%)
  local copies, waits for them, and re-layouts  0.6 us (2%)
    pallas_call x1, Pallas kernels, per_device(): pl.pallas_call(functools.partial(kernel, nb, nc, hs, tokens), out_shape=p...  30.4 us

profile of v2, /device:TPU:0, one launch (start us, length us, event | category | flops | bytes accessed | tf_op | source)
XLA Modules:
  0.0 31.0 jit_solution(6195927786220109828)
XLA Ops:
  0.0 30.4 %shard_map.82 = bf16[4,1024]{1,0:T(4,128)(2,1)S(1)} custom-call(bf16[1,4096]{1,0:T(2,128)(2,1)} %q_hbm.1, bf16[1,1024]{1,0:T(2,128)(2,1)} %nk_hbm.1, bf16[1,1024]{1,0:T(2,128)(2,1)} %nv_hbm.1, bf16[1,512,8,128]{3,2,1,0:T(8,128)(2,1)} %ck_hbm.1, bf16[1,512,8,128]{3,2,1,0:T(8,128)(2,1)} %cv_hbm.1, s32[4]{0:T(128)} %par_hbm.1, s32[4]{0:T(128)} %len_hbm.1, ...), custom_call_target="tpu_custom_call" | custom-call | tf_op jit(solution)/shard_map/pallas_call | solution.py:405
  30.4 0.6 %copy.10 = bf16[4,1024]{1,0:T(4,128)(2,1)} copy(bf16[4,1024]{1,0:T(4,128)(2,1)S(1)} %shard_map.82) | data formatting | bytes 16384

commit v3 on v1

--- a/solution.py
+++ b/solution.py
@@ -13,7 +13,7 @@
 HD = 128
 SPAN = 128
 GROUP = H // KVH
-MASKED = -1e30
+LOWEST = -3.0e38
 LANES = 128
 MESH = pl.DeviceIdType.MESH
 F32 = jnp.float32
@@ -187,9 +187,9 @@
             scores = lax.dot_general(
                 q, kh[kv_base + u], (((1,), (1,)), ((), ())), preferred_element_type=F32
             )
-            scores = jnp.where(usable, scores * scale, MASKED)
-            peak = jnp.max(scores, axis=1, keepdims=True)
-            weights = jnp.where(usable, jnp.exp(scores - peak), 0.0)
+            scores = jnp.where(usable, scores * scale, -jnp.inf)
+            peak = jnp.maximum(jnp.max(scores, axis=1, keepdims=True), LOWEST)
+            weights = jnp.exp(scores - peak)
             total = jnp.sum(weights, axis=1, keepdims=True)
             blended = jnp.dot(weights.astype(BF16), vh[kv_base + u], preferred_element_type=F32)
             d_send[s, u * ur : (u + 1) * ur, :] = blended.astype(BF16)
@@ -333,19 +333,11 @@
             device_id_type=MESH,
         )
 
-    chunk = min(512, quarter)
     for k in order:
         s = cmod(k)
         w_load(k).wait()
 
-        def multiply(i, carry):
-            n0 = pl.multiple_of(i * chunk, chunk)
-            g_send[s, :, pl.ds(n0, chunk)] = jnp.dot(
-                attended, w_vm[s, :, pl.ds(n0, chunk)], preferred_element_type=F32
-            )
-            return carry
-
-        lax.fori_loop(0, quarter // chunk, multiply, 0)
+        g_send[s] = jnp.dot(attended, w_vm[s], preferred_element_type=F32)
         if k:
             g_copy(k).start()
     total_out = g_send[c]
@@ -384,8 +376,8 @@
     dma = pltpu.SemaphoreType.DMA
     return pl.pallas_call(
         functools.partial(kernel, nb, nc, hs, rows, tokens),
-        out_shape=jax.ShapeDtypeStruct((nb, quarter), BF16),
-        in_specs=[pl.BlockSpec(memory_space=pl.ANY)] * 8,
+        out_shape=pltpu.VMEM((nb, quarter), BF16),
+        in_specs=[pl.BlockSpec(memory_space=pltpu.HBM)] * 8,
         out_specs=pl.BlockSpec(memory_space=pltpu.VMEM),
         scratch_shapes=[
             pltpu.VMEM((nc, depth, quarter), BF16),

time: 28.9 us -> 27.3 us (0.945)
  Pallas kernels: 27.2 us -> 26.2 us
  local copies, waits for them, and re-layouts: 1.3 us -> 0.6 us
    pallas_call x1, Pallas kernels: 27.2 us -> 26.2 us  [per_device(): pl.pallas_call(functools.partial(kernel, nb, nc, hs, rows, tokens), out_s...]
    unnamed x1, local copies, waits for them, and re-layouts: 1.3 us -> 0.6 us
where the time goes in v3:
time: 27.3 us; the launch traced here: 26.8 us
  Pallas kernels  26.2 us (96%)
  local copies, waits for them, and re-layouts  0.6 us (2%)
    pallas_call x1, Pallas kernels, per_device(): pl.pallas_call(functools.partial(kernel, nb, nc, hs, rows, tokens), out_s...  26.2 us
    unnamed x1, local copies, waits for them, and re-layouts  0.6 us

profile of v3, /device:TPU:0, one launch (start us, length us, event | category | flops | bytes accessed | tf_op | source)
XLA Modules:
  0.0 26.8 jit_solution(18029091440080570658)
XLA Ops:
  0.0 26.2 %shard_map.82 = bf16[4,1024]{1,0:T(4,128)(2,1)S(1)} custom-call(bf16[1,4096]{1,0:T(2,128)(2,1)} %q_hbm.1, bf16[1,1024]{1,0:T(2,128)(2,1)} %nk_hbm.1, bf16[1,1024]{1,0:T(2,128)(2,1)} %nv_hbm.1, bf16[1,512,8,128]{3,2,1,0:T(8,128)(2,1)} %ck_hbm.1, bf16[1,512,8,128]{3,2,1,0:T(8,128)(2,1)} %cv_hbm.1, s32[4]{0:T(128)} %par_hbm.1, s32[4]{0:T(128)} %len_hbm.1, ...), custom_call_target="tpu_custom_call" | custom-call | tf_op jit(solution)/shard_map/pallas_call | solution.py:377
  26.2 0.6 %copy.10 = bf16[4,1024]{1,0:T(4,128)(2,1)} copy(bf16[4,1024]{1,0:T(4,128)(2,1)S(1)} %shard_map.82) | data formatting | bytes 16384

commit v4 on v3

--- a/solution.py
+++ b/solution.py
@@ -158,15 +158,19 @@
 
     widen(ck_vm, k32)
     for kv in range(KVH):
-        kh[kv] = k32[pl.ds(kv, tokens, stride=KVH), :].astype(BF16)
+        u0 = (kv % units) * HD
+        kh[kv // units, :, u0 : u0 + HD] = k32[pl.ds(kv, tokens, stride=KVH), :].astype(BF16)
     loads[6].wait()
     widen(cv_vm, v32)
     for kv in range(KVH):
-        vh[kv] = v32[pl.ds(kv, tokens, stride=KVH), :].astype(BF16)
+        u0 = (kv % units) * HD
+        vh[kv // units, u0 : u0 + HD, :] = jnp.transpose(
+            v32[pl.ds(kv, tokens, stride=KVH), :].astype(BF16)
+        )
     loads[3].wait()
     loads[4].wait()
     limit = len_sm[p] * SPAN
-    position = c * tokens + lax.broadcasted_iota(jnp.int32, (ur, tokens), 1)
+    position = c * tokens + lax.broadcasted_iota(jnp.int32, (tokens, LANES), 0)
     usable = position < limit
     scale = 1.0 / math.sqrt(HD)
     lane_u = lax.broadcasted_iota(jnp.int32, (ur, LANES), 1)
@@ -176,29 +180,35 @@
     def to_lanes(column, u):
         return jnp.sum(jnp.where(lane_u == row_u + u * ur, column, 0.0), axis=0, keepdims=True)
 
+    lane_d = lax.broadcasted_iota(jnp.int32, (HD, LANES), 1)
+
     def attend(s):
-        kv_base = (s * hs) // GROUP
-        peak_row = jnp.zeros((1, LANES), F32)
-        sum_row = jnp.zeros((1, LANES), F32)
+        pair = (s * hs) // GROUP // units
+        bands = []
         for u in range(units):
             q = jnp.concatenate(
                 [q_buf[s, b, u * GROUP : (u + 1) * GROUP, :] for b in range(nb)], axis=0
             )
-            scores = lax.dot_general(
-                q, kh[kv_base + u], (((1,), (1,)), ((), ())), preferred_element_type=F32
+            bands.append(
+                jnp.concatenate([q if v == u else jnp.zeros_like(q) for v in range(units)], axis=1)
             )
-            scores = jnp.where(usable, scores * scale, -jnp.inf)
-            peak = jnp.maximum(jnp.max(scores, axis=1, keepdims=True), LOWEST)
-            weights = jnp.exp(scores - peak)
-            total = jnp.sum(weights, axis=1, keepdims=True)
-            blended = jnp.dot(weights.astype(BF16), vh[kv_base + u], preferred_element_type=F32)
-            d_send[s, u * ur : (u + 1) * ur, :] = blended.astype(BF16)
-            peak_row = peak_row + to_lanes(peak, u)
-            sum_row = sum_row + to_lanes(total, u)
+        scores = lax.dot_general(
+            kh[pair], jnp.concatenate(bands, axis=0), (((1,), (1,)), ((), ())),
+            preferred_element_type=F32,
+        )
+        scores = jnp.where(usable, scores * scale, -jnp.inf)
+        peak = jnp.maximum(jnp.max(scores, axis=0, keepdims=True), LOWEST)
+        weights = jnp.exp(scores - peak)
+        total = jnp.sum(weights, axis=0, keepdims=True)
+        both = jnp.dot(vh[pair], weights.astype(BF16), preferred_element_type=F32)
+        blended = both[0:HD]
+        for u in range(1, units):
+            blended = jnp.where(lane_d >= u * ur, both[u * HD : (u + 1) * HD], blended)
+        d_send[s, 0:HD, :] = blended.astype(BF16)
         stats = jnp.zeros((16, LANES), F32)
-        for i, piece in enumerate(split3(peak_row) + split3(sum_row)):
+        for i, piece in enumerate(split3(peak) + split3(total)):
             stats = jnp.where(row16 == i, piece, stats)
-        d_send[s, units * ur : units * ur + 16, :] = stats.astype(BF16)
+        d_send[s, HD : HD + 16, :] = stats.astype(BF16)
 
     def d_copy(k):
         return pltpu.make_async_remote_copy(
@@ -251,16 +261,15 @@
             jnp.broadcast_to(jnp.concatenate(own_scores, axis=0), (ur, LANES)), u
         )
     own_row = own_row * scale
-    own_value = jnp.concatenate(own_values, axis=0)
+    own_value = jnp.transpose(jnp.concatenate(own_values, axis=0))
 
     for k in range(1, nc):
         d_arrival(cmod(k)).wait_recv()
-    rows = units * ur
     states = []
     for k in range(nc):
         ref = d_send if k == 0 else d_recv
         s = cmod(k)
-        stats = ref[s, rows : rows + 16, :].astype(F32)
+        stats = ref[s, HD : HD + 16, :].astype(F32)
         states.append(
             (
                 ref, s,
@@ -279,17 +288,10 @@
         scales.append(factor)
         total = total + weight_sum * factor
     inverse = 1.0 / total
-    lane_r = lax.broadcasted_iota(jnp.int32, (rows, LANES), 1)
-    row_r = lax.broadcasted_iota(jnp.int32, (rows, LANES), 0)
-    diagonal = lane_r == row_r
-
-    def to_rows(lanes):
-        return jnp.sum(jnp.where(diagonal, lanes, 0.0), axis=1, keepdims=True)
-
-    result = own_value * to_rows(own_scale * inverse)
+    result = own_value * (own_scale * inverse)
     for (ref, s, _, _), factor in zip(states, scales):
-        result = result + ref[s, 0:rows, :].astype(F32) * to_rows(factor * inverse)
-    e_buf[p] = result.astype(BF16)
+        result = result + ref[s, 0:HD, :].astype(F32) * (factor * inverse)
+    e_buf[p] = jnp.transpose(result).astype(BF16)
 
     def e_copy(j):
         return pltpu.make_async_remote_copy(
@@ -370,7 +372,8 @@
     hs = queries.shape[1] // HD
     tokens = cache_keys.shape[1]
     rp = max(hs, GROUP)
-    rows = (rp // GROUP) * nb * GROUP
+    units = rp // GROUP
+    rows = units * nb * GROUP
     depth, columns = out_weight.shape
     quarter = columns // nc
     dma = pltpu.SemaphoreType.DMA
@@ -385,8 +388,8 @@
             pltpu.VMEM((tokens, KVH, HD), BF16),
             pltpu.VMEM((tokens * KVH, HD), F32),
             pltpu.VMEM((tokens * KVH, HD), F32),
-            pltpu.VMEM((KVH, tokens, HD), BF16),
-            pltpu.VMEM((KVH, tokens, HD), BF16),
+            pltpu.VMEM((KVH // units, tokens, units * HD), BF16),
+            pltpu.VMEM((KVH // units, units * HD, tokens), BF16),
             pltpu.VMEM(queries.shape, BF16),
             pltpu.VMEM(new_keys.shape, BF16),
             pltpu.VMEM(new_values.shape, BF16),
@@ -395,8 +398,8 @@
             pltpu.VMEM((rp, HD), F32),
             pltpu.VMEM((nc, nb, rp, HD), BF16),
             pltpu.VMEM((nb, 16, HD), BF16),
-            pltpu.VMEM((nc, rows + 16, HD), BF16),
-            pltpu.VMEM((nc, rows + 16, HD), BF16),
+            pltpu.VMEM((nc, HD + 16, rows), BF16),
+            pltpu.VMEM((nc, HD + 16, rows), BF16),
             pltpu.VMEM((nb, rows, HD), BF16),
             pltpu.VMEM((rows, HD), F32),
             pltpu.VMEM((nc, nb, quarter), F32),

time: 27.3 us -> 27.1 us (level)
  no operation moved by 1% of the time
where the time goes in v4:
time: 27.1 us; the launch traced here: 26.6 us
  Pallas kernels  26 us (96%)
  local copies, waits for them, and re-layouts  0.6 us (2%)
    pallas_call x1, Pallas kernels, per_device(): pl.pallas_call(functools.partial(kernel, nb, nc, hs, rows, tokens), out_s...  26 us
    unnamed x1, local copies, waits for them, and re-layouts  0.6 us

profile of v4, /device:TPU:0, one launch (start us, length us, event | category | flops | bytes accessed | tf_op | source)
XLA Modules:
  0.0 26.6 jit_solution(2306656035405146456)
XLA Ops:
  0.0 26.0 %shard_map.82 = bf16[4,1024]{1,0:T(4,128)(2,1)S(1)} custom-call(bf16[1,4096]{1,0:T(2,128)(2,1)} %q_hbm.1, bf16[1,1024]{1,0:T(2,128)(2,1)} %nk_hbm.1, bf16[1,1024]{1,0:T(2,128)(2,1)} %nv_hbm.1, bf16[1,512,8,128]{3,2,1,0:T(8,128)(2,1)} %ck_hbm.1, bf16[1,512,8,128]{3,2,1,0:T(8,128)(2,1)} %cv_hbm.1, s32[4]{0:T(128)} %par_hbm.1, s32[4]{0:T(128)} %len_hbm.1, ...), custom_call_target="tpu_custom_call" | custom-call | tf_op jit(solution)/shard_map/pallas_call | solution.py:380
  26.0 0.6 %copy.10 = bf16[4,1024]{1,0:T(4,128)(2,1)} copy(bf16[4,1024]{1,0:T(4,128)(2,1)S(1)} %shard_map.82) | data formatting | bytes 16384

commit v5 on v4

--- a/solution.py
+++ b/solution.py
@@ -48,7 +48,7 @@
         return (g, b, s)
 
     def cmod(k):
-        return lax.rem(c + k, nc)
+        return 2 * lax.rem(c // 2 + k // 2, nc // 2) + lax.rem(c + k, 2)
 
     def pmod(j):
         return lax.rem(p + j, nb)
@@ -61,9 +61,9 @@
             (ck_hbm.at[0], ck_vm), (cv_hbm.at[0], cv_vm),
         )
     ):
-        load = pltpu.make_async_copy(src, dst, in_sem.at[i])
+        loads.append(pltpu.make_async_copy(src, dst, in_sem.at[i]))
+    for load in loads[:3]:
         load.start()
-        loads.append(load)
 
     def w_load(k):
         s = cmod(k)
@@ -73,9 +73,7 @@
             w_sem.at[k],
         )
 
-    order = [k for k in range(1, nc)] + [0]
-    for k in order:
-        w_load(k).start()
+    order = [k for k in range(nc - 1, -1, -1)]
 
     barrier = pltpu.get_barrier_semaphore()
 
@@ -86,6 +84,11 @@
         return carry
 
     lax.fori_loop(1, nb * nc, greet, 0)
+
+    for load in loads[5:] + loads[3:5]:
+        load.start()
+    for k in order:
+        w_load(k).start()
 
     for i in range(3):
         loads[i].wait()

time: 27.1 us -> 25.1 us (0.926)
  Pallas kernels: 26 us -> 24.3 us
    pallas_call x1, Pallas kernels: 26 us -> 24.3 us  [per_device(): pl.pallas_call(functools.partial(kernel, nb, nc, hs, rows, tokens), out_s...]
where the time goes in v5:
time: 25.1 us; the launch traced here: 24.9 us
  Pallas kernels  24.3 us (97%)
  local copies, waits for them, and re-layouts  0.6 us (2%)
    pallas_call x1, Pallas kernels, per_device(): pl.pallas_call(functools.partial(kernel, nb, nc, hs, rows, tokens), out_s...  24.3 us
    unnamed x1, local copies, waits for them, and re-layouts  0.6 us

profile of v5, /device:TPU:0, one launch (start us, length us, event | category | flops | bytes accessed | tf_op | source)
XLA Modules:
  0.0 24.9 jit_solution(16890980712529417765)
XLA Ops:
  0.0 24.3 %shard_map.82 = bf16[4,1024]{1,0:T(4,128)(2,1)S(1)} custom-call(bf16[1,4096]{1,0:T(2,128)(2,1)} %q_hbm.1, bf16[1,1024]{1,0:T(2,128)(2,1)} %nk_hbm.1, bf16[1,1024]{1,0:T(2,128)(2,1)} %nv_hbm.1, bf16[1,512,8,128]{3,2,1,0:T(8,128)(2,1)} %ck_hbm.1, bf16[1,512,8,128]{3,2,1,0:T(8,128)(2,1)} %cv_hbm.1, s32[4]{0:T(128)} %par_hbm.1, s32[4]{0:T(128)} %len_hbm.1, ...), custom_call_target="tpu_custom_call" | custom-call | tf_op jit(solution)/shard_map/pallas_call | solution.py:383
  24.3 0.6 %copy.10 = bf16[4,1024]{1,0:T(4,128)(2,1)} copy(bf16[4,1024]{1,0:T(4,128)(2,1)S(1)} %shard_map.82) | data formatting | bytes 16384
